TPU v7x, 128 devices: a whole 4x4x4 slice. The times are simulated.
128 devices in a mesh: seq: 32 (over x, z, core), head: 4 (over y).
Axes of the slice: x: 4, y: 4, z: 4, core: 2. Of those that a mesh axis runs over, the one named last changes fastest.
Arguments:
- tokens: bfloat16 [16384, 4096], P('seq', 'head'), may hold values from -80 to 80, as said below
- w_query: bfloat16 [4096, 2048], P(None, 'head'), may hold values from -0.09375 to 0.09375
- w_key: bfloat16 [4096, 2048], P(None, 'head'), may hold values from -0.09375 to 0.09375
- w_value: bfloat16 [4096, 2048], P(None, 'head'), may hold values from -0.09375 to 0.09375
- w_out: bfloat16 [2048, 4096], P('head'), may hold values from -0.125 to 0.125
- block_bucket: int32 [128], P('seq'), may hold values from 0 to 575, as said below
Outputs:
- attended: bfloat16 [16384, 4096], P('seq', 'head')
Inputs may be any that keep to these rules, and one draw needn't show every extreme that they name: `tokens`: hidden states of order one; a few rows may be far larger. `block_bucket`: no bucket holds more than 2 blocks, and some bucket holds exactly 2; an owner's buckets are numbered from its first id on and hold 2 blocks each except possibly its first and its last. The blocks of one index of seq belong to buckets of at most 1 block per owner, and some owner receives exactly 1 from every index of seq.
All inputs are finite; a program needn't handle non-finite values.
Results may differ from a plain program's by a relative error of at most 0.012.
The roundings to bfloat16 on the way count: a program that leaves them out, or rounds other values in their place, can miss the bound.
Values may be sent and summed in bfloat16 or wider, within the bound.
A program may use at most 128 MiB of HBM per device.

v0:
```python
import jax
import jax.numpy as jnp
from jax import lax
from jax.sharding import PartitionSpec as P

HDIM = 128
BMAX = 2


def in_blocks(array, dim, count):
    before, after = (array.shape[:dim], array.shape[dim + 1 :])
    return jnp.moveaxis(array.reshape(*before, count, -1, *after), dim, 0)


def piece_ends(length, count):
    turn = length // count
    if turn >= 8:
        turn -= turn % 8
    return [turn * k for k in range(1, count)]


def laid_out(blocks, dim):
    blocks = jnp.moveaxis(blocks, 0, dim)
    shape = blocks.shape
    return blocks.reshape(*shape[:dim], shape[dim] * shape[dim + 1], *shape[dim + 2 :])


def exchange_in_pieces(array, axis, pieces, split_dim, concat_dim):
    blocks = in_blocks(array, split_dim, lax.axis_size(axis))
    cut = max(range(1, max(2, blocks.ndim - 1)), key=lambda d: blocks.shape[d])
    finished = []
    for share in jnp.split(blocks, piece_ends(blocks.shape[cut], pieces), axis=cut):
        if share.size:
            finished.append(lax.all_to_all(share, axis, split_axis=0, concat_axis=0, tiled=True))
    return laid_out(jnp.concatenate(finished, axis=cut), concat_dim)


def key_lists(bucket, valid):
    count = bucket.shape[0]
    match = (bucket[:, None] == bucket[None, :]) & valid[None, :]
    rank = jnp.cumsum(match.astype(jnp.int32), axis=1) - 1
    picks = match[:, :, None] & (
        rank[:, :, None] == jnp.arange(BMAX, dtype=jnp.int32)[None, None, :]
    )
    places = jnp.arange(count, dtype=jnp.int32)[None, :, None]
    index = jnp.sum(jnp.where(picks, places, 0), axis=1)
    usable = jnp.any(picks, axis=1)
    return (index, usable)


def per_device(tokens, w_query, w_key, w_value, w_out, block_bucket):
    seq_count = lax.axis_size("seq")
    head_count = lax.axis_size("head")
    blocks_here = block_bucket.shape[0]
    tok_here = tokens.shape[0]
    block_len = tok_here // blocks_here
    capacity = (blocks_here + seq_count - 1) // seq_count
    slot_count = seq_count * capacity
    local_width = w_query.shape[1]
    heads_here = local_width // HDIM
    owned = seq_count * capacity // BMAX + 2
    piece = lax.all_gather(tokens, "head", axis=1, tiled=True)
    query, keys, values = tuple(
        (
            jnp.dot(piece, weight, preferred_element_type=jnp.float32)
            for weight in (w_query, w_key, w_value)
        )
    )
    packed = jnp.concatenate(
        [query.astype(jnp.bfloat16), keys.astype(jnp.bfloat16), values.astype(jnp.bfloat16)], axis=1
    )
    packed = packed.reshape(blocks_here, block_len, 3 * local_width)
    owner = block_bucket // owned
    places = jnp.arange(blocks_here, dtype=jnp.int32)
    earlier = (owner[:, None] == owner[None, :]) & (places[None, :] < places[:, None])
    rank = jnp.sum(earlier.astype(jnp.int32), axis=1)
    slot_of_block = owner * capacity + rank
    hits = slot_of_block[None, :] == jnp.arange(slot_count, dtype=jnp.int32)[:, None]
    source_index = jnp.sum(jnp.where(hits, places[None, :], 0), axis=1)
    filled = jnp.any(hits, axis=1)
    outgoing = jnp.take(packed, source_index, axis=0)
    outgoing_ids = jnp.where(filled, jnp.take(block_bucket, source_index), -1)
    arrived, arrived_ids = (
        exchange_in_pieces(outgoing, "seq", 2, 0, 0),
        exchange_in_pieces(outgoing_ids, "seq", 2, 0, 0),
    )
    index, usable = key_lists(arrived_ids, arrived_ids >= 0)
    mask = jnp.repeat(usable, block_len, axis=1)

    def head_attend(which):
        query_head = lax.dynamic_slice_in_dim(arrived, which * HDIM, HDIM, 2)
        key_head = lax.dynamic_slice_in_dim(arrived, local_width + which * HDIM, HDIM, 2)
        value_head = lax.dynamic_slice_in_dim(arrived, 2 * local_width + which * HDIM, HDIM, 2)
        key_rows = jnp.take(key_head, index, axis=0).reshape(slot_count, BMAX * block_len, HDIM)
        value_rows = jnp.take(value_head, index, axis=0).reshape(slot_count, BMAX * block_len, HDIM)
        scores = jnp.einsum(
            "sqd,skd->sqk", query_head, key_rows, preferred_element_type=jnp.float32
        ) * HDIM ** (-0.5)
        scores = jnp.where(mask[:, None, :], scores, -1e30)
        top = jnp.max(scores, axis=-1, keepdims=True)
        expo = jnp.exp(scores - top)
        weights = (expo / jnp.sum(expo, axis=-1, keepdims=True)).astype(jnp.bfloat16)
        mixed = jnp.einsum("sqk,skd->sqd", weights, value_rows, preferred_element_type=jnp.float32)
        return mixed.astype(jnp.bfloat16)

    per_head = lax.map(head_attend, jnp.arange(heads_here, dtype=jnp.int32))
    results = jnp.transpose(per_head, (1, 2, 0, 3)).reshape(slot_count, block_len, local_width)
    returned = lax.all_to_all(results, "seq", split_axis=0, concat_axis=0, tiled=True)
    mixed_here = jnp.take(returned, slot_of_block, axis=0).reshape(tok_here, local_width)
    column_width = w_out.shape[1] // head_count
    rows_split = w_out.reshape(local_width, head_count, column_width)
    columns = lax.all_to_all(rows_split, "head", split_axis=1, concat_axis=0, tiled=True)
    columns = columns.reshape(head_count * local_width, column_width)
    summed = jnp.dot(
        lax.all_gather(mixed_here, "head", axis=1, tiled=True),
        columns,
        preferred_element_type=jnp.float32,
    )
    return summed.astype(jnp.bfloat16)


def solution(mesh):
    placed = (
        P("seq", "head"),
        P(None, "head"),
        P(None, "head"),
        P(None, "head"),
        P("head", None),
        P("seq"),
    )
    return jax.shard_map(
        per_device, mesh=mesh, in_specs=placed, out_specs=P("seq", "head"), check_vma=False
    )
```

profile of v0, /device:TPU:0, one launch (start us, length us, event | category | flops | bytes accessed | tf_op | source)
XLA Modules:
  0.0 513.7 jit_solution(11713508505914483083)
XLA Ops:
  13.6 8.2 %all-to-all-start = ((s32[32,1,1]{2,1,0:T(1,128)}), s32[32,1,1]{2,1,0:T(1,128)S(1)}, u32[]{:S(2)}, u32[]{:S(2)}) async-start(s32[32,1,1]{2,1,0:T(1,128)} %copy.33), calls=%async_computation | async-start | bytes 32768 | tf_op jit(solution)/shard_map/all_to_all | solution.py:34
  21.9 37.8 %all-gather.3.cloned.1.call-done = bf16[512,4096]{1,0:T(8,128)(2,1)} async-done(((bf16[512,1024]{1,0:T(8,128)(2,1)}), bf16[512,4096]{1,0:T(8,128)(2,1)}) %all-gather.3.cloned.1.call-update) | async-done | bytes 4194320 | tf_op jit(solution)/shard_map/all_gather | solution.py:62
  59.8 6.0 %convolution_convert_fusion.1 = bf16[512,512]{0,1:T(8,128)(2,1)S(1)} fusion(bf16[512,4096]{1,0:T(8,128)(2,1)} %all-gather.3.cloned.1.call-done, bf16[4096,512]{1,0:T(8,128)(2,1)} %param.13), kind=kOutput, calls=%fused_computation.36 | convolution fusion | flops 2147745792 | bytes 8912896 | tf_op jit(solution)/shard_map/dot_general | solution.py:65
  71.4 6.4 %gather_fusion.2 = bf16[32,128,1536]{2,1,0:T(8,128)(2,1)} fusion(bf16[4,128,1536]{2,1,0:T(8,128)(2,1)S(1)} %bitcast.85, s32[1024]{0:T(1024)S(1)} %pad_clamp_fusion.2), kind=kCustom, calls=%fused_computation.2 | custom fusion | bytes 25165952 | tf_op jit(solution)/shard_map/jit(_take)/gather | solution.py:81
  77.8 6.5 %bitcast_select_fusion = bf16[32,1,128,1536]{3,2,0,1:T(8,128)(2,1)S(1)} fusion(bf16[32,128,1536]{2,1,0:T(8,128)(2,1)} %gather_fusion.2, pred[32]{0:T(512)(128)(4,1)S(1)} %compare_and_fusion.2), kind=kLoop, calls=%fused_computation.31 | loop fusion | flops 6291456 | bytes 25165856 | tf_op jit(solution)/shard_map/jit(_take)/select_n | solution.py:81
  84.3 4.9 slice_bitcast_fusion.1
  89.3 80.4 %all_to_all.36 = bf16[32,1,64,1536]{3,2,1,0:T(8,128)(2,1)} all-to-all(bf16[32,1,64,1536]{3,2,1,0:T(8,128)(2,1)} %get-tuple-element.126), channel_id=1, replica_groups=mesh['seq'=32,'head'=4] {'seq'}, dimensions={0} | all-to-all | bytes 12582912 | tf_op jit(solution)/shard_map/all_to_all | solution.py:34
  169.6 5.1 all-to-all-start.2
  176.1 78.4 %all-to-all-done.2 = bf16[32,1,64,1536]{3,2,1,0:T(8,128)(2,1)} async-done(((bf16[32,1,64,1536]{3,2,1,0:T(8,128)(2,1)}), bf16[32,1,64,1536]{3,2,1,0:T(8,128)(2,1)}, u32[]{:S(2)}, u32[]{:S(2)}) %all-to-all-start.2) | async-done | bytes 6291488 | tf_op jit(solution)/shard_map/all_to_all | solution.py:34
  254.5 10.6 %maximum_bitcast_fusion = bf16[32,128,1536]{2,1,0:T(8,128)(2,1)} fusion(bf16[32,1,64,1536]{3,2,1,0:T(8,128)(2,1)} %all-to-all-done.2, bf16[32,1,64,1536]{3,2,1,0:T(8,128)(2,1)} %all_to_all.36), kind=kLoop, calls=%fused_computation.30 | loop fusion | flops 25165824 | bytes 25165824 | tf_op jit(solution)/shard_map/reshape | solution.py:25
  265.1 94.5 %while.13 = (s32[]{:T(128)}, bf16[4,32,128,128]{2,3,0,1:T(8,128)(2,1)}, s32[4]{0:T(128)S(1)}, bf16[32,128,1536]{2,1,0:T(8,128)(2,1)}, s32[32,2]{1,0:T(8,128)S(1)...) while((s32[]{:T(128)}, ...), condition=%wide.region_9.11_spmd.clone, body=%wide.region_6.10_spmd.clone.sunk | while | flops 547882816 | bytes 65084444 | solution.py:106
  279.3 6.5 %fusion.44 = (f32[32,128]{1,0:T(8,128)S(1)}, f32[32,128,256]{2,1,0:T(8,128)S(1)}) fusion(f32[32,128,256]{2,1,0:T(8,128)S(1)} %fusion.43, pred[32,256]{1,0:T(8,128)(4,1)S(1)} %bitcast.91), kind=kOutput, calls=%fused_computation.71.clone.1 | output fusion | flops 6291711 | bytes 8413184 | tf_op jit(solution)/shard_map/while/body/eval_jaxpr/sub | solution.py:101
  302.9 6.5 %fusion.44 = (f32[32,128]{1,0:T(8,128)S(1)}, f32[32,128,256]{2,1,0:T(8,128)S(1)}) fusion(f32[32,128,256]{2,1,0:T(8,128)S(1)} %fusion.43, pred[32,256]{1,0:T(8,128)(4,1)S(1)} %bitcast.91), kind=kOutput, calls=%fused_computation.71.clone.1 | output fusion | flops 6291711 | bytes 8413184 | tf_op jit(solution)/shard_map/while/body/eval_jaxpr/sub | solution.py:101
  319.8 4.0 broadcast_select_fusion.3
  326.6 6.5 %fusion.44 = (f32[32,128]{1,0:T(8,128)S(1)}, f32[32,128,256]{2,1,0:T(8,128)S(1)}) fusion(f32[32,128,256]{2,1,0:T(8,128)S(1)} %fusion.43, pred[32,256]{1,0:T(8,128)(4,1)S(1)} %bitcast.91), kind=kOutput, calls=%fused_computation.71.clone.1 | output fusion | flops 6291711 | bytes 8413184 | tf_op jit(solution)/shard_map/while/body/eval_jaxpr/sub | solution.py:101
  343.4 4.0 broadcast_select_fusion.3
  350.2 6.5 %fusion.44 = (f32[32,128]{1,0:T(8,128)S(1)}, f32[32,128,256]{2,1,0:T(8,128)S(1)}) fusion(f32[32,128,256]{2,1,0:T(8,128)S(1)} %fusion.43, pred[32,256]{1,0:T(8,128)(4,1)S(1)} %bitcast.91), kind=kOutput, calls=%fused_computation.71.clone.1 | output fusion | flops 6291711 | bytes 8413184 | tf_op jit(solution)/shard_map/while/body/eval_jaxpr/sub | solution.py:101
  359.7 11.3 %all-to-all-start.3 = ((bf16[32,128,512]{1,2,0:T(8,128)(2,1)}), bf16[32,128,512]{1,2,0:T(8,128)(2,1)}, u32[]{:S(2)}, u32[]{:S(2)}) async-start(bf16[32,128,512]{1,2,0:T(8,128)(2,1)} %bitcast.88), calls=%async_computation.3 | async-start | bytes 8388608 | tf_op jit(solution)/shard_map/all_to_all | solution.py:108
  370.9 6.5 %copy.38 = bf16[512,4096]{0,1:T(8,128)(2,1)} copy(bf16[512,4096]{1,0:T(8,128)(2,1)} %param.14) | data formatting | bytes 8388608 | tf_op args[4]
  377.6 46.1 %all-to-all-done.3 = bf16[32,128,512]{1,2,0:T(8,128)(2,1)} async-done(((bf16[32,128,512]{1,2,0:T(8,128)(2,1)}), bf16[32,128,512]{1,2,0:T(8,128)(2,1)}, u32[]{:S(2)}, u32[]{:S(2)}) %all-to-all-start.3) | async-done | bytes 4194336 | tf_op jit(solution)/shard_map/all_to_all | solution.py:108
  423.7 4.9 all-to-all-start.4
  432.6 61.8 %all-to-all-done.4 = bf16[512,4,1024]{0,2,1:T(8,128)(2,1)} async-done(((bf16[512,4,1024]{0,2,1:T(8,128)(2,1)}), bf16[512,4,1024]{0,2,1:T(8,128)(2,1)}, u32[]{:S(2)}, u32[]{:S(2)}) %all-to-all-start.4) | async-done | bytes 4194336 | tf_op jit(solution)/shard_map/all_to_all | solution.py:112
  494.4 6.3 %copy.39 = bf16[4,512,1,1024]{3,1,0,2:T(8,128)(2,1)} copy(bf16[4,512,1,1024]{1,3,0,2:T(8,128)(2,1)} %bitcast.20) | data formatting | bytes 8388608 | tf_op jit(solution)/shard_map/all_to_all | solution.py:112
  500.7 6.1 %convolution_convert_fusion = bf16[512,1024]{1,0:T(8,128)(2,1)} fusion(bf16[512,2048]{1,0:T(8,128)(2,1)} %all-gather.5.cloned.1.call-done, bf16[2048,1024]{1,0:T(8,128)(2,1)} %bitcast.89), kind=kOutput, calls=%fused_computation.35 | convolution fusion | flops 2148007936 | bytes 7340032 | tf_op jit(solution)/shard_map/dot_general | solution.py:114
  (118 shorter events, 75.9 us)
Async XLA Ops:
  6.5 53.2 %all-gather.3.cloned.1.call-start = ((), (), s32[]{:S(2)}) async-start(), calls=%async_computation.5 | async-start | bytes 5242880 | tf_op jit(solution)/shard_map/all_gather | solution.py:62
  13.6 75.6 %all-to-all-start = ((s32[32,1,1]{2,1,0:T(1,128)}), s32[32,1,1]{2,1,0:T(1,128)S(1)}, u32[]{:S(2)}, u32[]{:S(2)}) async-start(s32[32,1,1]{2,1,0:T(1,128)} %copy.33), calls=%async_computation | async-start | bytes 32768 | tf_op jit(solution)/shard_map/all_to_all | solution.py:34
  59.8 6.0 %copy-start.2 = (bf16[4096,512]{1,0:T(8,128)(2,1)S(1)}, bf16[4096,512]{1,0:T(8,128)(2,1)}, u32[]{:S(2)}) copy-start(bf16[4096,512]{1,0:T(8,128)(2,1)} %param.12) | copy-start | bytes 12582916
  59.8 6.0 %copy-start.4 = (bf16[512,4096]{1,0:T(8,128)(2,1)S(1)}, bf16[512,4096]{1,0:T(8,128)(2,1)}, u32[]{:S(2)}) copy-start(bf16[512,4096]{1,0:T(8,128)(2,1)} %all-gather.3.cloned.1.call-done) | copy-start | bytes 12582916
  65.8 2.4 copy-start.3
  169.6 84.9 %all-to-all-start.2 = ((bf16[32,1,64,1536]{3,2,1,0:T(8,128)(2,1)}), bf16[32,1,64,1536]{3,2,1,0:T(8,128)(2,1)}, u32[]{:S(2)}, u32[]{:S(2)}) async-start(bf16[32,1,64,1536]{3,2,1,0:T(8,128)(2,1)} %get-tuple-element.127), calls=%async_computation.2 | async-start | bytes 12582912 | tf_op jit(solution)/shard_map/all_to_all | solution.py:34
  270.3 2.2 copy-start
  279.3 6.5 %copy-start.1 = (bf16[32,2,128,128]{3,2,1,0:T(8,128)(2,1)S(1)}, bf16[32,2,128,128]{3,2,1,0:T(8,128)(2,1)}, u32[]{:S(2)}) copy-start(bf16[32,2,128,128]{3,2,1,0:T(8,128)(2,1)} %get-tuple-element.179) | copy-start | bytes 6291460 | tf_op jit(solution)/shard_map/while
  294.0 2.2 copy-start
  302.9 6.5 %copy-start.1 = (bf16[32,2,128,128]{3,2,1,0:T(8,128)(2,1)S(1)}, bf16[32,2,128,128]{3,2,1,0:T(8,128)(2,1)}, u32[]{:S(2)}) copy-start(bf16[32,2,128,128]{3,2,1,0:T(8,128)(2,1)} %get-tuple-element.179) | copy-start | bytes 6291460 | tf_op jit(solution)/shard_map/while
  317.6 2.2 copy-start
  326.6 6.5 %copy-start.1 = (bf16[32,2,128,128]{3,2,1,0:T(8,128)(2,1)S(1)}, bf16[32,2,128,128]{3,2,1,0:T(8,128)(2,1)}, u32[]{:S(2)}) copy-start(bf16[32,2,128,128]{3,2,1,0:T(8,128)(2,1)} %get-tuple-element.179) | copy-start | bytes 6291460 | tf_op jit(solution)/shard_map/while
  341.2 2.2 copy-start
  350.2 6.5 %copy-start.1 = (bf16[32,2,128,128]{3,2,1,0:T(8,128)(2,1)S(1)}, bf16[32,2,128,128]{3,2,1,0:T(8,128)(2,1)}, u32[]{:S(2)}) copy-start(bf16[32,2,128,128]{3,2,1,0:T(8,128)(2,1)} %get-tuple-element.179) | copy-start | bytes 6291460 | tf_op jit(solution)/shard_map/while
  359.7 64.0 %all-to-all-start.3 = ((bf16[32,128,512]{1,2,0:T(8,128)(2,1)}), bf16[32,128,512]{1,2,0:T(8,128)(2,1)}, u32[]{:S(2)}, u32[]{:S(2)}) async-start(bf16[32,128,512]{1,2,0:T(8,128)(2,1)} %bitcast.88), calls=%async_computation.3 | async-start | bytes 8388608 | tf_op jit(solution)/shard_map/all_to_all | solution.py:108
  423.7 70.7 %all-to-all-start.4 = ((bf16[512,4,1024]{0,2,1:T(8,128)(2,1)}), bf16[512,4,1024]{0,2,1:T(8,128)(2,1)}, u32[]{:S(2)}, u32[]{:S(2)}) async-start(bf16[512,4,1024]{0,2,1:T(8,128)(2,1)} %bitcast.87), calls=%async_computation.4 | async-start | bytes 8388608 | tf_op jit(solution)/shard_map/all_to_all | solution.py:112
  428.5 72.2 %all-gather.5.cloned.1.call-start = ((), (), s32[]{:S(2)}) async-start(), calls=%async_computation.6 | async-start | bytes 2621440 | tf_op jit(solution)/shard_map/all_gather | solution.py:115
Sparse Core Ops, SparseCore 0:
  9.0 50.6 all-gather.2
  432.7 48.4 all-gather.4
where the time goes:
time: 515 us; the launch traced here: 514 us
  waiting for transfers between devices  225 us (44%)
  blocking collectives  80.4 us (16%)
  other arithmetic  65.6 us (13%)
  local copies, waits for them, and re-layouts  65.2 us (13%)
  matrix products  31.7 us (6%)
  starting transfers between devices  29.5 us (6%)
  between operations  13.6 us (3%)
    all_to_all x1, blocking collectives, exchange_in_pieces(): lax.all_to_all(share, axis, split_axis=0, concat_axis=0, tiled=True)  80.4 us
    all_to_all x2, waiting for transfers between devices, exchange_in_pieces(): lax.all_to_all(share, axis, split_axis=0, concat_axis=0, tiled=True)  78.4 us
    all_to_all x1, waiting for transfers between devices, per_device(): lax.all_to_all(rows_split, 'head', split_axis=1, concat_axis=0, tiled=True)  61.8 us
    all_to_all x1, waiting for transfers between devices, per_device(): lax.all_to_all(results, 'seq', split_axis=0, concat_axis=0, tiled=True)  46.1 us
    all_gather x1, waiting for transfers between devices, per_device(): piece = lax.all_gather(tokens, 'head', axis=1, tiled=True)  37.8 us
    sub x4, other arithmetic, head_attend(): expo = jnp.exp(scores - top)  25.9 us
    select_n x8, other arithmetic, head_attend(): jnp.take(key_head, index, axis=0)  16 us
    all_to_all x2, starting transfers between devices, exchange_in_pieces(): lax.all_to_all(share, axis, split_axis=0, concat_axis=0, tiled=True)  13.3 us
  transfers between devices with their start and end apart: 6, of which 4 were waited for; matrix products, arithmetic and copies ran while one was open for 11% of the time, Pallas kernels for 0%

commit v1 on v0

--- a/solution.py
+++ b/solution.py
@@ -59,7 +59,10 @@
     local_width = w_query.shape[1]
     heads_here = local_width // HDIM
     owned = seq_count * capacity // BMAX + 2
-    piece = lax.all_gather(tokens, "head", axis=1, tiled=True)
+    size = lax.axis_size("head")
+    parts = jnp.stack([tokens for _ in range(size)])
+    parts = lax.all_to_all(parts, "head", split_axis=0, concat_axis=0)
+    piece = jnp.concatenate(parts, axis=1)
     query, keys, values = tuple(
         (
             jnp.dot(piece, weight, preferred_element_type=jnp.float32)

time: 515 us -> 533 us (1.035)
  waiting for transfers between devices: 225 us -> 231 us
    all_to_all x0 -> x1, waiting for transfers between devices: none -> 45 us  [per_device(): parts = lax.all_to_all(parts, 'head', split_axis=0, concat_axis=0)]
    all_gather x1 -> x0, waiting for transfers between devices: 37.8 us -> none  [per_device(): piece = lax.all_gather(tokens, 'head', axis=1, tiled=True)]
where the time goes in v1:
time: 533 us; the launch traced here: 531 us
  waiting for transfers between devices  231 us (43%)
  blocking collectives  80.5 us (15%)
  local copies, waits for them, and re-layouts  68.1 us (13%)
  other arithmetic  64.3 us (12%)
  matrix products  36.3 us (7%)
  starting transfers between devices  34.5 us (6%)
  between operations  13.6 us (3%)
    all_to_all x1, blocking collectives, exchange_in_pieces(): lax.all_to_all(share, axis, split_axis=0, concat_axis=0, tiled=True)  80.5 us
    all_to_all x2, waiting for transfers between devices, exchange_in_pieces(): lax.all_to_all(share, axis, split_axis=0, concat_axis=0, tiled=True)  78.4 us
    all_to_all x1, waiting for transfers between devices, per_device(): lax.all_to_all(rows_split, 'head', split_axis=1, concat_axis=0, tiled=True)  61.8 us
    all_to_all x1, waiting for transfers between devices, per_device(): lax.all_to_all(results, 'seq', split_axis=0, concat_axis=0, tiled=True)  46.1 us
    all_to_all x1, waiting for transfers between devices, per_device(): parts = lax.all_to_all(parts, 'head', split_axis=0, concat_axis=0)  45 us
    sub x4, other arithmetic, head_attend(): expo = jnp.exp(scores - top)  25.9 us
    select_n x8, other arithmetic, head_attend(): jnp.take(key_head, index, axis=0)  16.1 us
    dot_general x3, matrix products, per_device(): jnp.dot(piece, weight, preferred_element_type=jnp.float32)  15.3 us
  transfers between devices with their start and end apart: 6, of which 4 were waited for; matrix products, arithmetic and copies ran while one was open for 11% of the time, Pallas kernels for 0%

profile of v1, /device:TPU:0, one launch (start us, length us, event | category | flops | bytes accessed | tf_op | source)
XLA Modules:
  0.0 531.3 jit_solution(6744115863212240218)
XLA Ops:
  10.3 5.0 all-to-all-start.1
  19.5 45.0 %all-to-all-done.1 = bf16[4,512,1024]{1,2,0:T(8,128)(2,1)} async-done(((bf16[4,512,1024]{1,2,0:T(8,128)(2,1)}), bf16[4,512,1024]{1,2,0:T(8,128)(2,1)}, u32[]{:S(2)}, u32[]{:S(2)}) %all-to-all-start.1) | async-done | bytes 4194336 | tf_op jit(solution)/shard_map/all_to_all | solution.py:64
  64.5 8.2 %all-to-all-start = ((s32[32,1,1]{2,1,0:T(1,128)}), s32[32,1,1]{2,1,0:T(1,128)S(1)}, u32[]{:S(2)}, u32[]{:S(2)}) async-start(s32[32,1,1]{2,1,0:T(1,128)} %copy.38), calls=%async_computation | async-start | bytes 32768 | tf_op jit(solution)/shard_map/all_to_all | solution.py:34
  72.7 6.0 %convolution_convert_fusion.1 = bf16[512,512]{0,1:T(8,128)(2,1)S(1)} fusion(bf16[512,4096]{0,1:T(8,128)(2,1)} %bitcast.2, bf16[4096,512]{1,0:T(8,128)(2,1)} %param.13), kind=kOutput, calls=%fused_computation.36 | convolution fusion | flops 2147745792 | bytes 8912896 | tf_op jit(solution)/shard_map/dot_general | solution.py:68
  78.7 4.8 convolution_convert_fusion.2
  88.9 6.4 %gather_fusion.2 = bf16[32,128,1536]{2,1,0:T(8,128)(2,1)} fusion(bf16[4,128,1536]{2,1,0:T(8,128)(2,1)S(1)} %bitcast.88, s32[1024]{0:T(1024)S(1)} %pad_clamp_fusion.2), kind=kCustom, calls=%fused_computation.2 | custom fusion | bytes 25165952 | tf_op jit(solution)/shard_map/jit(_take)/gather | solution.py:84
  95.4 6.5 %bitcast_select_fusion = bf16[32,1,128,1536]{3,2,0,1:T(8,128)(2,1)S(1)} fusion(bf16[32,128,1536]{2,1,0:T(8,128)(2,1)} %gather_fusion.2, pred[32]{0:T(512)(128)(4,1)S(1)} %compare_and_fusion.2), kind=kLoop, calls=%fused_computation.31 | loop fusion | flops 6291456 | bytes 25165856 | tf_op jit(solution)/shard_map/jit(_take)/select_n | solution.py:84
  101.9 4.9 slice_bitcast_fusion.1
  106.9 80.5 %all_to_all.41 = bf16[32,1,64,1536]{3,2,1,0:T(8,128)(2,1)} all-to-all(bf16[32,1,64,1536]{3,2,1,0:T(8,128)(2,1)} %get-tuple-element.126), channel_id=1, replica_groups=mesh['seq'=32,'head'=4] {'seq'}, dimensions={0} | all-to-all | bytes 12582912 | tf_op jit(solution)/shard_map/all_to_all | solution.py:34
  187.3 5.1 all-to-all-start.3
  193.8 78.4 %all-to-all-done.3 = bf16[32,1,64,1536]{3,2,1,0:T(8,128)(2,1)} async-done(((bf16[32,1,64,1536]{3,2,1,0:T(8,128)(2,1)}), bf16[32,1,64,1536]{3,2,1,0:T(8,128)(2,1)}, u32[]{:S(2)}, u32[]{:S(2)}) %all-to-all-start.3) | async-done | bytes 6291488 | tf_op jit(solution)/shard_map/all_to_all | solution.py:34
  272.2 10.6 %maximum_bitcast_fusion = bf16[32,128,1536]{2,1,0:T(8,128)(2,1)} fusion(bf16[32,1,64,1536]{3,2,1,0:T(8,128)(2,1)} %all-to-all-done.3, bf16[32,1,64,1536]{3,2,1,0:T(8,128)(2,1)} %all_to_all.41), kind=kLoop, calls=%fused_computation.30 | loop fusion | flops 25165824 | bytes 25165824 | tf_op jit(solution)/shard_map/reshape | solution.py:25
  282.8 94.5 %while.13 = (s32[]{:T(128)}, bf16[4,32,128,128]{2,3,0,1:T(8,128)(2,1)}, s32[4]{0:T(128)S(1)}, bf16[32,128,1536]{2,1,0:T(8,128)(2,1)}, s32[32,2]{1,0:T(8,128)S(1)...) while((s32[]{:T(128)}, ...), condition=%wide.region_9.11_spmd.clone, body=%wide.region_6.10_spmd.clone.sunk | while | flops 547882816 | bytes 65084444 | solution.py:109
  297.0 6.5 %fusion.44 = (f32[32,128]{1,0:T(8,128)S(1)}, f32[32,128,256]{2,1,0:T(8,128)S(1)}) fusion(f32[32,128,256]{2,1,0:T(8,128)S(1)} %fusion.43, pred[32,256]{1,0:T(8,128)(4,1)S(1)} %bitcast.94), kind=kOutput, calls=%fused_computation.71.clone.1 | output fusion | flops 6291711 | bytes 8413184 | tf_op jit(solution)/shard_map/while/body/eval_jaxpr/sub | solution.py:104
  320.7 6.5 %fusion.44 = (f32[32,128]{1,0:T(8,128)S(1)}, f32[32,128,256]{2,1,0:T(8,128)S(1)}) fusion(f32[32,128,256]{2,1,0:T(8,128)S(1)} %fusion.43, pred[32,256]{1,0:T(8,128)(4,1)S(1)} %bitcast.94), kind=kOutput, calls=%fused_computation.71.clone.1 | output fusion | flops 6291711 | bytes 8413184 | tf_op jit(solution)/shard_map/while/body/eval_jaxpr/sub | solution.py:104
  344.3 6.5 %fusion.44 = (f32[32,128]{1,0:T(8,128)S(1)}, f32[32,128,256]{2,1,0:T(8,128)S(1)}) fusion(f32[32,128,256]{2,1,0:T(8,128)S(1)} %fusion.43, pred[32,256]{1,0:T(8,128)(4,1)S(1)} %bitcast.94), kind=kOutput, calls=%fused_computation.71.clone.1 | output fusion | flops 6291711 | bytes 8413184 | tf_op jit(solution)/shard_map/while/body/eval_jaxpr/sub | solution.py:104
  367.9 6.5 %fusion.44 = (f32[32,128]{1,0:T(8,128)S(1)}, f32[32,128,256]{2,1,0:T(8,128)S(1)}) fusion(f32[32,128,256]{2,1,0:T(8,128)S(1)} %fusion.43, pred[32,256]{1,0:T(8,128)(4,1)S(1)} %bitcast.94), kind=kOutput, calls=%fused_computation.71.clone.1 | output fusion | flops 6291711 | bytes 8413184 | tf_op jit(solution)/shard_map/while/body/eval_jaxpr/sub | solution.py:104
  377.4 11.3 %all-to-all-start.4 = ((bf16[32,128,512]{1,2,0:T(8,128)(2,1)}), bf16[32,128,512]{1,2,0:T(8,128)(2,1)}, u32[]{:S(2)}, u32[]{:S(2)}) async-start(bf16[32,128,512]{1,2,0:T(8,128)(2,1)} %bitcast.91), calls=%async_computation.4 | async-start | bytes 8388608 | tf_op jit(solution)/shard_map/all_to_all | solution.py:111
  388.6 6.6 %copy.43 = bf16[512,4096]{0,1:T(8,128)(2,1)} copy(bf16[512,4096]{1,0:T(8,128)(2,1)} %param.14) | data formatting | bytes 8388608 | tf_op args[4]
  395.3 46.1 %all-to-all-done.4 = bf16[32,128,512]{1,2,0:T(8,128)(2,1)} async-done(((bf16[32,128,512]{1,2,0:T(8,128)(2,1)}), bf16[32,128,512]{1,2,0:T(8,128)(2,1)}, u32[]{:S(2)}, u32[]{:S(2)}) %all-to-all-start.4) | async-done | bytes 4194336 | tf_op jit(solution)/shard_map/all_to_all | solution.py:111
  441.4 4.9 all-to-all-start.5
  450.3 61.8 %all-to-all-done.5 = bf16[512,4,1024]{0,2,1:T(8,128)(2,1)} async-done(((bf16[512,4,1024]{0,2,1:T(8,128)(2,1)}), bf16[512,4,1024]{0,2,1:T(8,128)(2,1)}, u32[]{:S(2)}, u32[]{:S(2)}) %all-to-all-start.5) | async-done | bytes 4194336 | tf_op jit(solution)/shard_map/all_to_all | solution.py:115
  512.0 6.3 %copy.44 = bf16[4,512,1,1024]{3,1,0,2:T(8,128)(2,1)} copy(bf16[4,512,1,1024]{1,3,0,2:T(8,128)(2,1)} %bitcast.23) | data formatting | bytes 8388608 | tf_op jit(solution)/shard_map/all_to_all | solution.py:115
  518.4 6.1 %convolution_convert_fusion = bf16[512,1024]{1,0:T(8,128)(2,1)} fusion(bf16[512,2048]{1,0:T(8,128)(2,1)} %all-gather.2.cloned.1.call-done, bf16[2048,1024]{1,0:T(8,128)(2,1)} %bitcast.92), kind=kOutput, calls=%fused_computation.35 | convolution fusion | flops 2148007936 | bytes 7340032 | tf_op jit(solution)/shard_map/dot_general | solution.py:117
  (119 shorter events, 84.6 us)
Async XLA Ops:
  10.3 5.0 copy-start.2
  10.3 54.2 %all-to-all-start.1 = ((bf16[4,512,1024]{1,2,0:T(8,128)(2,1)}), bf16[4,512,1024]{1,2,0:T(8,128)(2,1)}, u32[]{:S(2)}, u32[]{:S(2)}) async-start(bf16[4,512,1024]{1,2,0:T(8,128)(2,1)} %stack.2), calls=%async_computation.1 | async-start | bytes 8388608 | tf_op jit(solution)/shard_map/all_to_all | solution.py:64
  64.5 42.4 %all-to-all-start = ((s32[32,1,1]{2,1,0:T(1,128)}), s32[32,1,1]{2,1,0:T(1,128)S(1)}, u32[]{:S(2)}, u32[]{:S(2)}) async-start(s32[32,1,1]{2,1,0:T(1,128)} %copy.38), calls=%async_computation | async-start | bytes 32768 | tf_op jit(solution)/shard_map/all_to_all | solution.py:34
  72.7 6.0 %copy-start.3 = (bf16[4096,512]{1,0:T(8,128)(2,1)S(1)}, bf16[4096,512]{1,0:T(8,128)(2,1)}, u32[]{:S(2)}) copy-start(bf16[4096,512]{1,0:T(8,128)(2,1)} %param.12) | copy-start | bytes 12582916
  78.7 4.8 copy-start.4
  187.3 84.8 %all-to-all-start.3 = ((bf16[32,1,64,1536]{3,2,1,0:T(8,128)(2,1)}), bf16[32,1,64,1536]{3,2,1,0:T(8,128)(2,1)}, u32[]{:S(2)}, u32[]{:S(2)}) async-start(bf16[32,1,64,1536]{3,2,1,0:T(8,128)(2,1)} %get-tuple-element.127), calls=%async_computation.3 | async-start | bytes 12582912 | tf_op jit(solution)/shard_map/all_to_all | solution.py:34
  288.0 2.2 copy-start
  297.0 6.5 %copy-start.1 = (bf16[32,2,128,128]{3,2,1,0:T(8,128)(2,1)S(1)}, bf16[32,2,128,128]{3,2,1,0:T(8,128)(2,1)}, u32[]{:S(2)}) copy-start(bf16[32,2,128,128]{3,2,1,0:T(8,128)(2,1)} %get-tuple-element.179) | copy-start | bytes 6291460 | tf_op jit(solution)/shard_map/while
  311.7 2.2 copy-start
  320.7 6.5 %copy-start.1 = (bf16[32,2,128,128]{3,2,1,0:T(8,128)(2,1)S(1)}, bf16[32,2,128,128]{3,2,1,0:T(8,128)(2,1)}, u32[]{:S(2)}) copy-start(bf16[32,2,128,128]{3,2,1,0:T(8,128)(2,1)} %get-tuple-element.179) | copy-start | bytes 6291460 | tf_op jit(solution)/shard_map/while
  335.3 2.2 copy-start
  344.3 6.5 %copy-start.1 = (bf16[32,2,128,128]{3,2,1,0:T(8,128)(2,1)S(1)}, bf16[32,2,128,128]{3,2,1,0:T(8,128)(2,1)}, u32[]{:S(2)}) copy-start(bf16[32,2,128,128]{3,2,1,0:T(8,128)(2,1)} %get-tuple-element.179) | copy-start | bytes 6291460 | tf_op jit(solution)/shard_map/while
  358.9 2.2 copy-start
  367.9 6.5 %copy-start.1 = (bf16[32,2,128,128]{3,2,1,0:T(8,128)(2,1)S(1)}, bf16[32,2,128,128]{3,2,1,0:T(8,128)(2,1)}, u32[]{:S(2)}) copy-start(bf16[32,2,128,128]{3,2,1,0:T(8,128)(2,1)} %get-tuple-element.179) | copy-start | bytes 6291460 | tf_op jit(solution)/shard_map/while
  377.4 64.0 %all-to-all-start.4 = ((bf16[32,128,512]{1,2,0:T(8,128)(2,1)}), bf16[32,128,512]{1,2,0:T(8,128)(2,1)}, u32[]{:S(2)}, u32[]{:S(2)}) async-start(bf16[32,128,512]{1,2,0:T(8,128)(2,1)} %bitcast.91), calls=%async_computation.4 | async-start | bytes 8388608 | tf_op jit(solution)/shard_map/all_to_all | solution.py:111
  441.4 70.7 %all-to-all-start.5 = ((bf16[512,4,1024]{0,2,1:T(8,128)(2,1)}), bf16[512,4,1024]{0,2,1:T(8,128)(2,1)}, u32[]{:S(2)}, u32[]{:S(2)}) async-start(bf16[512,4,1024]{0,2,1:T(8,128)(2,1)} %bitcast.90), calls=%async_computation.5 | async-start | bytes 8388608 | tf_op jit(solution)/shard_map/all_to_all | solution.py:115
  446.2 72.1 %all-gather.2.cloned.1.call-start = ((), (), s32[]{:S(2)}) async-start(), calls=%async_computation.6 | async-start | bytes 2621440 | tf_op jit(solution)/shard_map/all_gather | solution.py:118
Sparse Core Ops, SparseCore 0:
  450.4 48.4 all-gather.1
